TPU v7x, 512 devices: a whole 4x4x16 slice. The times are simulated.
512 devices in a mesh: row: 32 (over z, y_hi), col: 16 (over x, y_lo, core).
Axes of the slice: x: 4, y: 4 (y_hi: 2, y_lo: 2; y = y_hi * 2 + y_lo), z: 16, core: 2. Of those that a mesh axis runs over, the one named last changes fastest.
Arguments:
- blocks: float32 [32, 16, 8, 128, 128], P('row', 'col'), may hold values from -1.2 to 1.2
- block_rows: int32 [32, 16, 8], P('row', 'col'), may hold values from -1 to 15, as said below
- block_cols: int32 [32, 16, 8], P('row', 'col'), may hold values from -1 to 31, as said below
Outputs:
- square_part: float32 [32, 16, 8, 128, 128], P('row', 'col')
Inputs may be any that keep to these rules, and one draw needn't show every extreme that they name: Empty slots have -1 in block_rows and block_cols alike; a used slot has a block row below 16; no block is listed twice in one tile. At most 4 used slots of one tile share a block row, and some tile has a block row with exactly 4. Some tile uses all 8 slots, and some tile has empty slots. `block_cols`: the two lists describe the same slots; a used slot has a block column below 32.
All inputs are finite; a program needn't handle non-finite values.
Results may differ from a plain program's by a relative error of at most 0.0003.
Values sent between devices are 32-bit elements; how exact they have to be, the bound alone decides.
A program may use at most 64 MiB of HBM per device.

v0:
```python
import jax
import jax.numpy as jnp
from jax import lax
from jax.sharding import PartitionSpec as P

NBLK = 512
ACT = 2
SECTIONS = 4


def from_root(x, axis, root):
    mine = lax.axis_index(axis) == root
    return lax.psum(jnp.where(mine, x, jnp.zeros_like(x)), axis)


def from_partner(x, axis, bit):
    return lax.ppermute(x, axis, [(i, i ^ 1 << bit) for i in range(lax.axis_size(axis))])


def shifted(value, axis, steps):
    count = lax.axis_size(axis)
    pairs = [(source, (source + steps) % count) for source in range(count)]
    return lax.ppermute(value, axis, pairs)


def section_product(panel, pair, out_rows, out_cols, depth):
    panel_vals, panel_rows, panel_cols = panel
    pair_vals, pair_inner, pair_cols = pair
    panel_iota = jnp.arange(panel_rows.shape[0], dtype=jnp.int32)
    pair_iota = jnp.arange(pair_inner.shape[0], dtype=jnp.int32)
    depth_iota = jnp.arange(depth, dtype=jnp.int32)
    panel_live = panel_rows >= 0
    earlier = (
        (panel_rows[None, :] == panel_rows[:, None])
        & panel_live[None, :]
        & (panel_iota[None, :] < panel_iota[:, None])
    )
    within = jnp.sum(earlier.astype(jnp.int32), axis=1)
    picked = (panel_rows[None, None, :] == out_rows[:, None, None]) & (
        within[None, None, :] == depth_iota[None, :, None]
    )
    picked = picked & panel_live[None, None, :] & (out_rows >= 0)[:, None, None]
    picked_int = picked.astype(jnp.int32)
    panel_slot = jnp.sum(picked_int * panel_iota[None, None, :], axis=2)
    found = jnp.sum(picked_int, axis=2) > 0
    inner = jnp.sum(picked_int * panel_cols[None, None, :], axis=2)
    matched = (pair_inner[None, None, :] == inner[:, :, None]) & (
        pair_cols[None, None, :] == out_cols[:, None, None]
    )
    matched = matched & (pair_inner >= 0)[None, None, :] & found[:, :, None]
    matched_int = matched.astype(jnp.int32)
    pair_slot = jnp.sum(matched_int * pair_iota[None, None, :], axis=2)
    weight = (jnp.sum(matched_int, axis=2) > 0).astype(jnp.float32)
    left = panel_vals[panel_slot] * weight[:, :, None, None]
    right = pair_vals[pair_slot]
    return jnp.einsum(
        "tqij,tqjk->tik",
        left,
        right,
        precision=lax.Precision.HIGHEST,
        preferred_element_type=jnp.float32,
    )


def make_pair(first, second, row_span):
    inner = jnp.concatenate([first[1], jnp.where(second[1] >= 0, second[1] + row_span, -1)])
    return (jnp.concatenate([first[0], second[0]]), inner, jnp.concatenate([first[2], second[2]]))


def order_pair(mine, other, is_even, row_span):
    first = tuple((jnp.where(is_even, one, two) for one, two in zip(mine, other)))
    second = tuple((jnp.where(is_even, two, one) for one, two in zip(mine, other)))
    return make_pair(first, second, row_span)


def fetch_panel(tile, row_index, col_count, section):
    root = (row_index // 2 + section) % col_count
    return (
        from_root(tile[0], "col", root),
        from_root(tile[1], "col", root),
        from_root(tile[2], "col", root),
    )


def body(blocks, block_rows, block_cols):
    tile = (blocks[0, 0], block_rows[0, 0], block_cols[0, 0])
    row_count = lax.axis_size("row")
    col_count = lax.axis_size("col")
    row_span = NBLK // row_count
    row_index = lax.axis_index("row")
    is_even = row_index % 2 == 0
    depth = 2 * ACT
    total = jnp.zeros(blocks.shape[2:], jnp.float32)
    partner = from_partner((tile[0], tile[1], tile[2]), "row", 0)
    start_pair = order_pair(tile, partner, is_even, row_span)
    current = start_pair
    for section in range(SECTIONS):
        panel = fetch_panel(tile, row_index, col_count, section)
        if section > 0:
            current = shifted((current[0], current[1], current[2]), "row", -2)
        total = total + section_product(panel, current, tile[1], tile[2], depth)
    return total[None, None]


def solution(mesh):
    return jax.shard_map(
        body,
        mesh=mesh,
        in_specs=(P("row", "col", None, None, None), P("row", "col", None), P("row", "col", None)),
        out_specs=P("row", "col", None, None, None),
        check_vma=False,
    )
```

profile of v0, /device:TPU:1, one launch (start us, length us, event | category | flops | bytes accessed | tf_op | source)
XLA Modules:
  0.0 244.3 jit_solution(5052952195378283427)
XLA Ops:
  6.5 5.6 %collective-permute-start.2 = (f32[8,128,128]{2,1,0:T(8,128)}, f32[8,128,128]{2,1,0:T(8,128)S(1)}, u32[]{:S(2)}, u32[]{:S(2)}) collective-permute-start(f32[8,128,128]{2,1,0:T(8,128)} %bitcast.96), channel_id=1, source_target_pairs={{0,16},{16,0},{32,48},{48,32},{64,80},{80,64},{96,112},{112,96},{1... | collective-permute-start | bytes 1572872 | tf_op jit(solution)/shard_map/ppermute | solution.py:17
  14.1 4.9 %collective-permute-start.1 = (s32[8]{0:T(128)}, s32[8]{0:T(128)S(1)}, u32[]{:S(2)}, u32[]{:S(2)}) collective-permute-start(s32[8]{0:T(128)} %bitcast.99), channel_id=1, source_target_pairs={{0,16},{16,0},{32,48},{48,32},{64,80},{80,64},{96,112},{112,96},{1... | collective-permute-start | bytes 104 | tf_op jit(solution)/shard_map/ppermute | solution.py:17
  22.2 13.9 %all-reduce = (s32[8]{0:T(128)S(1)}, s32[8]{0:T(128)S(1)}, s32[8]{0:T(128)S(1)}, s32[8]{0:T(128)S(1)}, s32[8]{0:T(128)S(1)}, /*index=5*/s32[8]{0:T(128)S(1)}, s32[8]{0:T(128)S(1)}, s32[8]{0:T(128)S(1)}) all-reduce(s32[8]{0:T(128)S(1)} %get-tuple-element.71, s32[8]{0:T(128)S(1)} %get-tuple-element.67, ...), channel_id=1, replica_groups=mesh['row'=32,'col'=16] {'col'}, use_global_device_ids=true, to_apply=%region_28.29 | all-reduce | flops 64 | bytes 512 | tf_op jit(solution)/shard_map/psum | solution.py:13
  38.3 11.1 %collective-permute-start.4 = (s32[16]{0:T(128)S(1)}, s32[16]{0:T(128)S(1)}, u32[]{:S(2)}, u32[]{:S(2)}) collective-permute-start(s32[16]{0:T(128)S(1)} %pad_add_fusion.1), channel_id=1, source_target_pairs={{0,480},{16,496},{32,0},{48,16},{64,32},{80,48},{96,64},{112,80},{... | collective-permute-start | bytes 200 | tf_op jit(solution)/shard_map/ppermute | solution.py:23
  49.7 2.6 %collective-permute-start.3 = (s32[16]{0:T(128)S(1)}, s32[16]{0:T(128)S(1)}, u32[]{:S(2)}, u32[]{:S(2)}) collective-permute-start(s32[16]{0:T(128)S(1)} %get-tuple-element.47), channel_id=1, source_target_pairs={{0,480},{16,496},{32,0},{48,16},{64,32},{80,48},{96,64},{112,80},{... | collective-permute-start | bytes 200 | tf_op jit(solution)/shard_map/ppermute | solution.py:23
  53.0 2.6 %collective-permute-start.7 = (s32[16]{0:T(128)S(1)}, s32[16]{0:T(128)S(1)}, u32[]{:S(2)}, u32[]{:S(2)}) collective-permute-start(s32[16]{0:T(128)S(1)} %collective-permute-done.4), channel_id=1, source_target_pairs={{0,480},{16,496},{32,0},{48,16},{64,32},{80,48},{96,64},{112,80},{... | collective-permute-start | bytes 200 | tf_op jit(solution)/shard_map/ppermute | solution.py:23
  55.6 2.6 %collective-permute-start.6 = (s32[16]{0:T(128)S(1)}, s32[16]{0:T(128)S(1)}, u32[]{:S(2)}, u32[]{:S(2)}) collective-permute-start(s32[16]{0:T(128)S(1)} %collective-permute-done.3), channel_id=1, source_target_pairs={{0,480},{16,496},{32,0},{48,16},{64,32},{80,48},{96,64},{112,80},{... | collective-permute-start | bytes 200 | tf_op jit(solution)/shard_map/ppermute | solution.py:23
  58.3 3.8 %collective-permute-start.10 = (s32[16]{0:T(128)S(1)}, s32[16]{0:T(128)S(1)}, u32[]{:S(2)}, u32[]{:S(2)}) collective-permute-start(s32[16]{0:T(128)S(1)} %collective-permute-done.7), channel_id=1, source_target_pairs={{0,480},{16,496},{32,0},{48,16},{64,32},{80,48},{96,64},{112,80},{... | collective-permute-start | bytes 200 | tf_op jit(solution)/shard_map/ppermute | solution.py:23
  62.1 2.6 %collective-permute-start.9 = (s32[16]{0:T(128)S(1)}, s32[16]{0:T(128)S(1)}, u32[]{:S(2)}, u32[]{:S(2)}) collective-permute-start(s32[16]{0:T(128)S(1)} %collective-permute-done.6), channel_id=1, source_target_pairs={{0,480},{16,496},{32,0},{48,16},{64,32},{80,48},{96,64},{112,80},{... | collective-permute-start | bytes 200 | tf_op jit(solution)/shard_map/ppermute | solution.py:23
  65.9 2.4 broadcast_select_fusion
  68.4 2.8 %collective-permute-start.5 = (f32[16,128,128]{2,1,0:T(8,128)S(1)}, f32[16,128,128]{2,1,0:T(8,128)S(1)}, u32[]{:S(2)}, u32[]{:S(2)}) collective-permute-start(f32[16,128,128]{2,1,0:T(8,128)S(1)} %pad_maximum_fusion), channel_id=1, source_target_pairs={{0,480},{16,496},{32,0},{48,16},{64,32},{80,48},{96,64},{112,80},{... | collective-permute-start | bytes 3145736 | tf_op jit(solution)/shard_map/ppermute | solution.py:23
  72.6 17.6 %collective-permute-done.5 = f32[16,128,128]{2,1,0:T(8,128)S(1)} collective-permute-done((f32[16,128,128]{2,1,0:T(8,128)S(1)}, f32[16,128,128]{2,1,0:T(8,128)S(1)}, u32[]{:S(2)}, u32[]{:S(2)}) %collective-permute-start.5) | collective-permute-done | bytes 1048608 | tf_op jit(solution)/shard_map/ppermute | solution.py:23
  90.2 3.4 %collective-permute-start.8 = (f32[16,128,128]{2,1,0:T(8,128)S(1)}, f32[16,128,128]{2,1,0:T(8,128)}, u32[]{:S(2)}, u32[]{:S(2)}) collective-permute-start(f32[16,128,128]{2,1,0:T(8,128)S(1)} %collective-permute-done.5), channel_id=1, source_target_pairs={{0,480},{16,496},{32,0},{48,16},{64,32},{80,48},{96,64},{112,80},{... | collective-permute-start | bytes 3145736 | tf_op jit(solution)/shard_map/ppermute | solution.py:23
  94.2 17.7 %collective-permute-done.8 = f32[16,128,128]{2,1,0:T(8,128)} collective-permute-done((f32[16,128,128]{2,1,0:T(8,128)S(1)}, f32[16,128,128]{2,1,0:T(8,128)}, u32[]{:S(2)}, u32[]{:S(2)}) %collective-permute-start.8) | collective-permute-done | bytes 1048608 | tf_op jit(solution)/shard_map/ppermute | solution.py:23
  111.9 3.6 %collective-permute-start.11 = (f32[16,128,128]{2,1,0:T(8,128)}, f32[16,128,128]{2,1,0:T(8,128)}, u32[]{:S(2)}, u32[]{:S(2)}) collective-permute-start(f32[16,128,128]{2,1,0:T(8,128)} %collective-permute-done.8), channel_id=1, source_target_pairs={{0,480},{16,496},{32,0},{48,16},{64,32},{80,48},{96,64},{112,80},{... | collective-permute-start | bytes 3145736 | tf_op jit(solution)/shard_map/ppermute | solution.py:23
  118.2 89.4 %all-reduce.4.cloned.1.call-done = (f32[8,128,128]{2,1,0:T(8,128)}, f32[8,128,128]{2,1,0:T(8,128)}, f32[8,128,128]{2,1,0:T(8,128)}, f32[8,128,128]{2,1,0:T(8,128)}) async-done(((f32[8,128,128]{2,1,0:T(8,128)}, f32[8,128,128]{2,1,0:T(8,128)}, f32[8,128,128]{2,1,0:T(8,128)}, f32[8,128,128]{2,1,0:T(8,128)}), (f32[8,128,128]{2,1,0:T(8,128)}, f32[8,128,128]{2,1,0:T(8,128)}, f32[8,128,128]{2,1,0:T(8,128)}, ...) | async-done | bytes 2097168 | tf_op jit(solution)/shard_map/psum | solution.py:13
  207.6 3.1 %gather_fusion = f32[32,128,128]{2,1,0:T(8,128)} fusion(f32[8,128,128]{2,1,0:T(8,128)} %get-tuple-element.42, s32[1024]{0:T(1024)S(1)} %pad_clamp_fusion.7), kind=kCustom, calls=%fused_computation | custom fusion | bytes 4194432 | tf_op jit(solution)/shard_map/gather | solution.py:54
  212.7 2.1 gather_fusion.4
  216.8 3.2 %gather_fusion.5 = f32[32,128,128]{2,1,0:T(8,128)} fusion(f32[16,128,128]{2,1,0:T(8,128)} %collective-permute-done.8, s32[1024]{0:T(1024)S(1)} %pad_clamp_fusion.2), kind=kCustom, calls=%fused_computation.5 | custom fusion | bytes 4194432 | tf_op jit(solution)/shard_map/gather | solution.py:55
  220.0 4.7 %fusion.8 = f32[8,128,128]{2,1,0:T(8,128)S(1)} fusion(f32[8,4,128,128]{3,2,1,0:T(8,128)} %bitcast.94, f32[8,4,128,128]{3,2,1,0:T(8,128)} %bitcast.95, f32[8,4]{1,0:T(8,128)S(1)} %copy.21), kind=kOutput, calls=%fused_computation.16 | convolution fusion | flops 805830656 | bytes 4718720 | tf_op jit(solution)/shard_map/tqij,tqjk->tik/dot_general | solution.py:56
  224.8 2.4 fusion.29
  227.2 2.3 fusion.26
  229.5 3.4 %gather_fusion.7 = f32[32,128,128]{2,1,0:T(8,128)} fusion(f32[16,128,128]{2,1,0:T(8,128)} %collective-permute-done.11, s32[1024]{0:T(1024)S(1)} %pad_clamp_fusion), kind=kCustom, calls=%fused_computation.7 | custom fusion | bytes 4194432 | tf_op jit(solution)/shard_map/gather | solution.py:55
  232.9 4.6 %fusion.23 = f32[1,1,8,128,128]{4,3,2,1,0:T(8,128)} fusion(f32[8,128,128]{2,1,0:T(8,128)S(1)} %fusion.26, f32[8,4,128,128]{3,2,1,0:T(8,128)} %bitcast.93, f32[8,4,128,128]{3,2,1,0:T(8,128)S(1)} %bitcast.89, f32[8,4]{1,0:T(8,128)S(1)} %copy.30), kind=kOutput, calls=%fused_computation.21 | convolution fusion | flops 805961728 | bytes 5243008 | tf_op jit(solution)/shard_map/tqij,tqjk->tik/dot_general | solution.py:56
  (101 shorter events, 17.9 us)
Async XLA Ops:
  6.5 201.1 %all-reduce.4.cloned.1.call-start = ((), (), s32[]{:S(2)}) async-start(), calls=%async_computation | async-start | bytes 4194304 | tf_op jit(solution)/shard_map/psum | solution.py:13
  6.5 59.3 %collective-permute-start.2 = (f32[8,128,128]{2,1,0:T(8,128)}, f32[8,128,128]{2,1,0:T(8,128)S(1)}, u32[]{:S(2)}, u32[]{:S(2)}) collective-permute-start(f32[8,128,128]{2,1,0:T(8,128)} %bitcast.96), channel_id=1, source_target_pairs={{0,16},{16,0},{32,48},{48,32},{64,80},{80,64},{96,112},{112,96},{1... | collective-permute-start | bytes 1572872 | tf_op jit(solution)/shard_map/ppermute | solution.py:17
  12.2 8.6 %collective-permute-start = (s32[8]{0:T(128)}, s32[8]{0:T(128)S(1)}, u32[]{:S(2)}, u32[]{:S(2)}) collective-permute-start(s32[8]{0:T(128)} %bitcast.97), channel_id=1, source_target_pairs={{0,16},{16,0},{32,48},{48,32},{64,80},{80,64},{96,112},{112,96},{1... | collective-permute-start | bytes 104 | tf_op jit(solution)/shard_map/ppermute | solution.py:17
  14.1 7.4 %collective-permute-start.1 = (s32[8]{0:T(128)}, s32[8]{0:T(128)S(1)}, u32[]{:S(2)}, u32[]{:S(2)}) collective-permute-start(s32[8]{0:T(128)} %bitcast.99), channel_id=1, source_target_pairs={{0,16},{16,0},{32,48},{48,32},{64,80},{80,64},{96,112},{112,96},{1... | collective-permute-start | bytes 104 | tf_op jit(solution)/shard_map/ppermute | solution.py:17
  38.3 14.6 %collective-permute-start.4 = (s32[16]{0:T(128)S(1)}, s32[16]{0:T(128)S(1)}, u32[]{:S(2)}, u32[]{:S(2)}) collective-permute-start(s32[16]{0:T(128)S(1)} %pad_add_fusion.1), channel_id=1, source_target_pairs={{0,480},{16,496},{32,0},{48,16},{64,32},{80,48},{96,64},{112,80},{... | collective-permute-start | bytes 200 | tf_op jit(solution)/shard_map/ppermute | solution.py:23
  49.7 5.9 %collective-permute-start.3 = (s32[16]{0:T(128)S(1)}, s32[16]{0:T(128)S(1)}, u32[]{:S(2)}, u32[]{:S(2)}) collective-permute-start(s32[16]{0:T(128)S(1)} %get-tuple-element.47), channel_id=1, source_target_pairs={{0,480},{16,496},{32,0},{48,16},{64,32},{80,48},{96,64},{112,80},{... | collective-permute-start | bytes 200 | tf_op jit(solution)/shard_map/ppermute | solution.py:23
  53.0 5.3 %collective-permute-start.7 = (s32[16]{0:T(128)S(1)}, s32[16]{0:T(128)S(1)}, u32[]{:S(2)}, u32[]{:S(2)}) collective-permute-start(s32[16]{0:T(128)S(1)} %collective-permute-done.4), channel_id=1, source_target_pairs={{0,480},{16,496},{32,0},{48,16},{64,32},{80,48},{96,64},{112,80},{... | collective-permute-start | bytes 200 | tf_op jit(solution)/shard_map/ppermute | solution.py:23
  55.6 6.5 %collective-permute-start.6 = (s32[16]{0:T(128)S(1)}, s32[16]{0:T(128)S(1)}, u32[]{:S(2)}, u32[]{:S(2)}) collective-permute-start(s32[16]{0:T(128)S(1)} %collective-permute-done.3), channel_id=1, source_target_pairs={{0,480},{16,496},{32,0},{48,16},{64,32},{80,48},{96,64},{112,80},{... | collective-permute-start | bytes 200 | tf_op jit(solution)/shard_map/ppermute | solution.py:23
  58.3 6.5 %collective-permute-start.10 = (s32[16]{0:T(128)S(1)}, s32[16]{0:T(128)S(1)}, u32[]{:S(2)}, u32[]{:S(2)}) collective-permute-start(s32[16]{0:T(128)S(1)} %collective-permute-done.7), channel_id=1, source_target_pairs={{0,480},{16,496},{32,0},{48,16},{64,32},{80,48},{96,64},{112,80},{... | collective-permute-start | bytes 200 | tf_op jit(solution)/shard_map/ppermute | solution.py:23
  62.1 31.4 %collective-permute-start.9 = (s32[16]{0:T(128)S(1)}, s32[16]{0:T(128)S(1)}, u32[]{:S(2)}, u32[]{:S(2)}) collective-permute-start(s32[16]{0:T(128)S(1)} %collective-permute-done.6), channel_id=1, source_target_pairs={{0,480},{16,496},{32,0},{48,16},{64,32},{80,48},{96,64},{112,80},{... | collective-permute-start | bytes 200 | tf_op jit(solution)/shard_map/ppermute | solution.py:23
  68.4 21.8 %collective-permute-start.5 = (f32[16,128,128]{2,1,0:T(8,128)S(1)}, f32[16,128,128]{2,1,0:T(8,128)S(1)}, u32[]{:S(2)}, u32[]{:S(2)}) collective-permute-start(f32[16,128,128]{2,1,0:T(8,128)S(1)} %pad_maximum_fusion), channel_id=1, source_target_pairs={{0,480},{16,496},{32,0},{48,16},{64,32},{80,48},{96,64},{112,80},{... | collective-permute-start | bytes 3145736 | tf_op jit(solution)/shard_map/ppermute | solution.py:23
  90.2 21.7 %collective-permute-start.8 = (f32[16,128,128]{2,1,0:T(8,128)S(1)}, f32[16,128,128]{2,1,0:T(8,128)}, u32[]{:S(2)}, u32[]{:S(2)}) collective-permute-start(f32[16,128,128]{2,1,0:T(8,128)S(1)} %collective-permute-done.5), channel_id=1, source_target_pairs={{0,480},{16,496},{32,0},{48,16},{64,32},{80,48},{96,64},{112,80},{... | collective-permute-start | bytes 3145736 | tf_op jit(solution)/shard_map/ppermute | solution.py:23
  111.9 117.6 %collective-permute-start.11 = (f32[16,128,128]{2,1,0:T(8,128)}, f32[16,128,128]{2,1,0:T(8,128)}, u32[]{:S(2)}, u32[]{:S(2)}) collective-permute-start(f32[16,128,128]{2,1,0:T(8,128)} %collective-permute-done.8), channel_id=1, source_target_pairs={{0,480},{16,496},{32,0},{48,16},{64,32},{80,48},{96,64},{112,80},{... | collective-permute-start | bytes 3145736 | tf_op jit(solution)/shard_map/ppermute | solution.py:23
  207.6 3.1 %copy-start.2 = (f32[8,128,128]{2,1,0:T(8,128)S(1)}, f32[8,128,128]{2,1,0:T(8,128)}, u32[]{:S(2)}) copy-start(f32[8,128,128]{2,1,0:T(8,128)} %get-tuple-element.43) | copy-start | bytes 1572868
  210.7 2.0 copy-start.1
  212.7 2.1 copy-start
  220.0 4.7 %copy-start.5 = (f32[32,128,128]{2,1,0:T(8,128)S(1)}, f32[32,128,128]{2,1,0:T(8,128)}, u32[]{:S(2)}) copy-start(f32[32,128,128]{2,1,0:T(8,128)} %gather_fusion.2) | copy-start | bytes 6291460
  224.8 2.4 copy-start.4
  224.8 2.4 copy-start.6
  229.5 3.4 %copy-start.3 = (f32[32,128,128]{2,1,0:T(8,128)S(1)}, f32[32,128,128]{2,1,0:T(8,128)}, u32[]{:S(2)}) copy-start(f32[32,128,128]{2,1,0:T(8,128)} %gather_fusion.6) | copy-start | bytes 6291460
Sparse Core Ops, SparseCore 0:
  71.6 135.9 all-reduce.3
where the time goes:
time: 245 us; the launch traced here: 244 us
  waiting for transfers between devices  126 us (51%)
  starting transfers between devices  47.7 us (19%)
  local copies, waits for them, and re-layouts  20.2 us (8%)
  matrix products  14 us (6%)
  blocking collectives  13.9 us (6%)
  between operations  13.9 us (6%)
  other arithmetic  8.89 us (4%)
    psum x1, waiting for transfers between devices, from_root(): return lax.psum(jnp.where(mine, x, jnp.zeros_like(x)), axis)  89.4 us
    ppermute x9, waiting for transfers between devices, shifted(): return lax.ppermute(value, axis, pairs)  35.3 us
    ppermute x9, starting transfers between devices, shifted(): return lax.ppermute(value, axis, pairs)  35.2 us
    dot_general x4, matrix products, section_product(): jnp.einsum('tqij,tqjk->tik', left, right, precision=lax.Precision.HIGHEST...  14 us
    psum x1, blocking collectives, from_root(): return lax.psum(jnp.where(mine, x, jnp.zeros_like(x)), axis)  13.9 us
    ppermute x3, starting transfers between devices, from_partner(): lax.ppermute(x, axis, [(i, i ^ 1 << bit) for i in range(lax.axis_size(axi...  12.4 us
    gather x4, local copies, waits for them, and re-layouts, section_product(): right = pair_vals[pair_slot]  9.31 us
    gather x4, local copies, waits for them, and re-layouts, section_product(): left = panel_vals[panel_slot] * weight[:, :, None, None]  9.18 us
  transfers between devices with their start and end apart: 13, of which 4 were waited for; matrix products, arithmetic and copies ran while one was open for 14% of the time, Pallas kernels for 0%

commit v1 on v0

v1 whole, which is shorter than its diff:
```python
import functools

import jax
import jax.numpy as jnp
from jax import lax
from jax.experimental import pallas as pl
from jax.experimental.pallas import tpu as pltpu
from jax.sharding import PartitionSpec as P

MESH = pl.DeviceIdType.MESH
BS = 128
SLOTS = 8
RB = 16
SECTIONS = 4
VIA_Z = 4
F32 = jnp.float32


def gather_kernel(blocks, rows, cols, b_out, a_out, mb_out, ma_out, meta, local_sem,
                  zs, zr, ys, yr, mzs, mzr, mys, myr, rs, rr, rms, rmr, gs, gr, cs, cr):
    row, col = lax.axis_index("row"), lax.axis_index("col")
    z, yh = row // 2, row % 2
    other = 1 - yh
    x, yl, core = col // 4, (col // 2) % 2, col % 2
    below = ((z + 15) % 16 * 2 + yh, col)
    above = ((z + 1) % 16 * 2 + yh, col)
    partner = (z * 2 + other, col)
    section = (col + 16 - z) % 16
    is_root = section < SECTIONS
    chunk = x * 2 + core

    def remote(src, dst, send, recv, to):
        return pltpu.make_async_remote_copy(
            src_ref=src, dst_ref=dst, send_sem=send, recv_sem=recv, device_id=to, device_id_type=MESH
        )

    own = pltpu.make_async_copy(blocks, b_out.at[0, yh], local_sem.at[0])
    own.start()
    meta[...] = jnp.full((8, BS), -1, jnp.int32)
    meta[0:1, 0:SLOTS] = rows[...]
    meta[1:2, 0:SLOTS] = cols[...]
    own_meta = pltpu.make_async_copy(meta, mb_out.at[0, yh], local_sem.at[1])
    own_meta.start()

    barrier = pltpu.get_barrier_semaphore()
    for to in (below, above, partner):
        pl.semaphore_signal(barrier, inc=1, device_id=to, device_id_type=MESH)
    for d in range(1, 16):
        pl.semaphore_signal(barrier, inc=1, device_id=(row, (col + d) % 16), device_id_type=MESH)
    pl.semaphore_wait(barrier, 18)

    sends = []

    def go(copy):
        copy.start()
        sends.append(copy)

    go(remote(meta, mb_out.at[1, yh], mzs.at[0], mzr.at[0], below))
    go(remote(meta, mb_out.at[0, yh], mys.at[0], myr.at[0], partner))
    for q in range(SLOTS):
        go(remote(blocks.at[q], b_out.at[1, yh, q], zs.at[q], zr.at[q], below))
        go(remote(blocks.at[q], b_out.at[0, yh, q], ys.at[q], yr.at[q], partner))

    def root_copies():
        out = []
        for d in range(1, 16):
            c = (col + d) % 16
            b = c // 4 * 2 + c % 2
            out.append(remote(blocks.at[b], a_out.at[b, section], rs.at[d], rr.at[section], (row, c)))
            out.append(remote(meta, ma_out.at[section], rms.at[d], rmr.at[section], (row, c)))
        return out

    @pl.when(is_root)
    def _():
        for copy in root_copies():
            copy.start()
        mine = pltpu.make_async_copy(blocks.at[chunk], a_out.at[chunk, section], local_sem.at[2])
        mine.start()
        mine_meta = pltpu.make_async_copy(meta, ma_out.at[section], local_sem.at[3])
        mine_meta.start()
        mine.wait()
        mine_meta.wait()

    own.wait()
    own_meta.wait()

    def from_above(i):
        s, q = 1 + i // SLOTS, i % SLOTS
        return remote(blocks.at[q], b_out.at[s, yh, q], zs.at[i], zr.at[i], below)

    def panel_spread():
        for s in range(SECTIONS):
            @pl.when(section != s)
            def _():
                remote(blocks.at[0], a_out.at[chunk, s], rs.at[0], rr.at[s], partner).wait_recv()
                remote(meta, ma_out.at[s], rms.at[0], rmr.at[s], partner).wait_recv()
        for d in range(1, 4):
            to = (row, (x + d) % 4 * 4 + yl * 2 + core)
            go(remote(a_out.at[chunk], a_out.at[chunk], gs.at[d], gr.at[d], to))
        twin = (row, x * 4 + yl * 2 + 1 - core)
        go(remote(a_out.at[chunk], a_out.at[chunk], cs.at[0], cr.at[0], twin))

    def panel_twin():
        twin = (row, x * 4 + yl * 2 + 1 - core)
        for d in range(1, 4):
            b = (x + 4 - d) % 4 * 2 + core
            remote(a_out.at[b], a_out.at[b], gs.at[d], gr.at[d], twin).wait_recv()
            go(remote(a_out.at[b], a_out.at[b], cs.at[d], cr.at[d], twin))

    for i in range(24):
        s, q = 1 + i // SLOTS, i % SLOTS
        if q == 0:
            remote(meta, mb_out.at[s, yh], mzs.at[s - 1], mzr.at[s - 1], below).wait_recv()
            if s < SECTIONS - 1:
                go(remote(mb_out.at[s, yh], mb_out.at[s + 1, yh], mzs.at[s], mzr.at[s], below))
            go(remote(mb_out.at[s, yh], mb_out.at[s, yh], mys.at[s], myr.at[s], partner))
        from_above(i).wait_recv()
        if s < SECTIONS - 1:
            go(remote(b_out.at[s, yh, q], b_out.at[s + 1, yh, q], zs.at[i + 8], zr.at[i + 8], below))
        if s < SECTIONS - 1 or q < SLOTS - VIA_Z:
            go(remote(b_out.at[s, yh, q], b_out.at[s, yh, q], ys.at[s * 8 + q], yr.at[s * 8 + q], partner))
        if i == 10:
            panel_spread()

    def from_partner(s, q):
        return remote(blocks.at[q], b_out.at[s, other, q], ys.at[s * 8 + q], yr.at[s * 8 + q], partner)

    for v in range(VIA_Z):
        q = SLOTS - VIA_Z + v
        from_partner(2, q).wait_recv()
        go(remote(b_out.at[2, other, q], b_out.at[3, other, q], zs.at[24 + v], zr.at[24 + v], below))
    panel_twin()
    for s in range(SECTIONS):
        remote(meta, mb_out.at[s, other], mys.at[s], myr.at[s], partner).wait_recv()
        for q in range(SLOTS):
            if s == 2 and q >= SLOTS - VIA_Z:
                continue
            if s == 3 and q >= SLOTS - VIA_Z:
                v = q - (SLOTS - VIA_Z)
                remote(blocks.at[q], b_out.at[3, other, q], zs.at[24 + v], zr.at[24 + v], below).wait_recv()
            else:
                from_partner(s, q).wait_recv()
    twin = (row, x * 4 + yl * 2 + 1 - core)
    for d in range(4):
        b = (x + 4 - d) % 4 * 2 + 1 - core
        remote(a_out.at[b], a_out.at[b], cs.at[d], cr.at[d], twin).wait_recv()

    @pl.when(is_root)
    def _():
        for copy in root_copies():
            copy.wait_send()

    for copy in sends:
        copy.wait_send()


def product_kernel(rows, cols, b_in, a_in, mb, ma, out, table, table_s, sem):
    n = SLOTS
    diag = lax.broadcasted_iota(jnp.int32, (n, n), 0) == lax.broadcasted_iota(jnp.int32, (n, n), 1)

    def upright(line):
        wide = jnp.broadcast_to(line, (n, n))
        return jnp.sum(jnp.where(diag, wide, 0), axis=1, keepdims=True)

    out_rows = upright(rows[...])
    out_cols = upright(cols[...])
    for s in range(SECTIONS):
        a_rows = ma[s, 0:1, 0:n]
        a_cols = ma[s, 1:2, 0:n]
        same_row = (out_rows == a_rows) & (out_rows >= 0)
        found = jnp.full((n, n), -1, jnp.int32)
        for h in range(2):
            for q in range(n):
                inner = mb[s, h, 0:1, q:q + 1]
                b_col = mb[s, h, 1:2, q:q + 1]
                hit = (a_cols == inner + RB * h) & (out_cols == b_col) & (inner >= 0)
                found = jnp.where(hit & same_row, h * n + q, found)
        table[s * n:(s + 1) * n, 0:n] = found
    copy = pltpu.make_async_copy(table, table_s, sem)
    copy.start()
    out[...] = jnp.zeros_like(out)
    copy.wait()

    def step(i, carry):
        s, t, p = i // 64, (i // 8) % 8, i % 8
        where = table_s[i // 8, p]

        @pl.when(where >= 0)
        def _():
            a = a_in[p, s]
            b = b_in[s, where // n, where % n]
            a_hi = a.astype(jnp.bfloat16)
            a_lo = (a - a_hi.astype(F32)).astype(jnp.bfloat16)
            b_hi = b.astype(jnp.bfloat16)
            b_lo = (b - b_hi.astype(F32)).astype(jnp.bfloat16)
            left = jnp.concatenate([a_hi, a_lo], axis=1)
            right = jnp.concatenate(
                [jnp.concatenate([b_hi, b_lo], axis=1),
                 jnp.concatenate([b_hi, jnp.zeros_like(b_lo)], axis=1)], axis=0)
            both = jnp.dot(left, right, preferred_element_type=F32)
            out[t] += both[:, :BS] + both[:, BS:]

        return carry

    lax.fori_loop(0, SECTIONS * n * n, step, 0)


def body(blocks, block_rows, block_cols):
    x = blocks[0, 0]
    rows, cols = block_rows[0], block_cols[0]
    dma = pltpu.SemaphoreType.DMA
    hbm = pl.BlockSpec(memory_space=pl.ANY)
    vmem = pl.BlockSpec(memory_space=pltpu.VMEM)
    b_all, a_all, mb, ma = pl.pallas_call(
        gather_kernel,
        out_shape=(
            jax.ShapeDtypeStruct((SECTIONS, 2, SLOTS, BS, BS), F32),
            jax.ShapeDtypeStruct((SLOTS, SECTIONS, BS, BS), F32),
            jax.ShapeDtypeStruct((SECTIONS, 2, 8, BS), jnp.int32),
            jax.ShapeDtypeStruct((SECTIONS, 8, BS), jnp.int32),
        ),
        in_specs=[hbm, vmem, vmem],
        out_specs=(hbm, hbm, hbm, hbm),
        scratch_shapes=[
            pltpu.VMEM((8, BS), jnp.int32), dma((4,)),
            dma((28,)), dma((28,)), dma((32,)), dma((32,)),
            dma((3,)), dma((3,)), dma((4,)), dma((4,)),
            dma((16,)), dma((4,)), dma((16,)), dma((4,)),
            dma((4,)), dma((4,)), dma((4,)), dma((4,)),
        ],
        compiler_params=pltpu.CompilerParams(collective_id=0, has_side_effects=True),
        name="gather_tiles",
    )(x, rows, cols)
    out = pl.pallas_call(
        product_kernel,
        out_shape=jax.ShapeDtypeStruct((SLOTS, BS, BS), F32),
        in_specs=[vmem] * 6,
        out_specs=vmem,
        scratch_shapes=[
            pltpu.VMEM((SECTIONS * SLOTS, BS), jnp.int32),
            pltpu.SMEM((SECTIONS * SLOTS, BS), jnp.int32),
            dma(()),
        ],
        compiler_params=pltpu.CompilerParams(vmem_limit_bytes=32 * 2**20),
        name="matched_products",
    )(rows, cols, b_all, a_all, mb, ma)
    return out[None, None]


def solution(mesh):
    return jax.shard_map(
        body,
        mesh=mesh,
        in_specs=(P("row", "col", None, None, None), P("row", "col", None), P("row", "col", None)),
        out_specs=P("row", "col", None, None, None),
        check_vma=False,
    )
```

time: 245 us -> 76.5 us (0.31)
  waiting for transfers between devices: 126 us -> 0 us
  Pallas kernels: 0 us -> 69.6 us
  starting transfers between devices: 47.7 us -> 0 us
  matrix products: 14 us -> 0 us
  blocking collectives: 13.9 us -> 0 us
  between operations: 13.9 us -> 0.02 us
  local copies, waits for them, and re-layouts: 20.2 us -> 6.56 us
  other arithmetic: 8.89 us -> 0 us
    psum x1 -> x0, waiting for transfers between devices: 89.4 us -> none  [from_root(): return lax.psum(jnp.where(mine, x, jnp.zeros_like(x)), axis)]
    pallas_call x0 -> x2, Pallas kernels: none -> 69.6 us  [the longest x1 59.3 us: body(): pl.pallas_call(gather_kernel, out_shape=(jax.ShapeDtypeStruct((SECTIONS,...]
    ppermute x12 -> x0, starting transfers between devices: 47.7 us -> none  [the longest x9 35.2 us: shifted(): return lax.ppermute(value, axis, pairs)]
    ppermute x12 -> x0, waiting for transfers between devices: 36.4 us -> none  [the longest x9 35.3 us: shifted(): return lax.ppermute(value, axis, pairs)]
    gather x8 -> x0, local copies, waits for them, and re-layouts: 18.5 us -> none  [the longest x4 9.31 us: section_product(): right = pair_vals[pair_slot]]
    dot_general x4 -> x0, matrix products: 14 us -> none  [section_product(): jnp.einsum('tqij,tqjk->tik', left, right, precision=lax.Precision.HIGHEST...]
    psum x1 -> x0, blocking collectives: 13.9 us -> none  [from_root(): return lax.psum(jnp.where(mine, x, jnp.zeros_like(x)), axis)]
    unnamed x14 -> x12, local copies, waits for them, and re-layouts: 0.03 us -> 6.56 us
  transfers between devices with their start and end apart: 13 -> 0, of which waited for: 4 -> 0; matrix products, arithmetic and copies ran while one was open for 14% -> 0% of each run, Pallas kernels for 0% -> 0%
where the time goes in v1:
time: 76.5 us; the launch traced here: 76.1 us
  Pallas kernels  69.6 us (91%)
  local copies, waits for them, and re-layouts  6.56 us (9%)
    pallas_call x1, Pallas kernels, body(): pl.pallas_call(gather_kernel, out_shape=(jax.ShapeDtypeStruct((SECTIONS,...  59.3 us
    pallas_call x1, Pallas kernels, body(): pl.pallas_call(product_kernel, out_shape=jax.ShapeDtypeStruct((SLOTS, BS,...  10.2 us
    unnamed x12, local copies, waits for them, and re-layouts  6.56 us

profile of v1, /device:TPU:1, one launch (start us, length us, event | category | flops | bytes accessed | tf_op | source)
XLA Modules:
  0.0 76.1 jit_solution(4684684102287041418)
XLA Ops:
  0.0 59.3 %gather_tiles.1 = (f32[4,2,8,128,128]{4,3,2,1,0:T(8,128)}, f32[8,4,128,128]{3,2,1,0:T(8,128)}, s32[4,2,8,128]{3,2,1,0:T(8,128)}, s32[4,8,128]{2,1,0:T(8,128)}) custom-call(f32[8,128,128]{2,1,0:T(8,128)} %bitcast.8, s32[1,8]{1,0:T(1,128)} %bitcast.4, s32[1,8]{1,0:T(1,128)} %bitcast.6), custom_call_target="tpu_custom_call" | custom-call | tf_op jit(solution)/shard_map/gather_tiles/pallas_call | solution.py:214
  59.3 0.0 copy-start
  59.3 2.2 %copy-done = f32[4,2,8,128,128]{4,3,2,1,0:T(8,128)S(1)} copy-done((f32[4,2,8,128,128]{4,3,2,1,0:T(8,128)S(1)}, f32[4,2,8,128,128]{4,3,2,1,0:T(8,128)}, u32[]{:S(2)}) %copy-start) | copy-done | bytes 4194328
  61.5 0.0 copy-start.1
  61.5 1.6 %copy-done.1 = f32[8,4,128,128]{3,2,1,0:T(8,128)S(1)} copy-done((f32[8,4,128,128]{3,2,1,0:T(8,128)S(1)}, f32[8,4,128,128]{3,2,1,0:T(8,128)}, u32[]{:S(2)}) %copy-start.1) | copy-done | bytes 2097176
  63.1 0.0 copy-start.2
  63.1 0.8 copy-done.2
  63.9 0.0 copy-start.3
  63.9 0.7 copy-done.3
  64.6 0.0 copy-start.4
  64.6 0.7 copy-done.4
  65.2 0.0 copy-start.5
  65.2 0.7 copy-done.5
  65.9 10.2 %matched_products.1 = f32[8,128,128]{2,1,0:T(8,128)} custom-call(s32[1,8]{1,0:T(1,128)S(1)} %bitcast.5, s32[1,8]{1,0:T(1,128)S(1)} %bitcast.7, f32[4,2,8,128,128]{4,3,2,1,0:T(8,128)S(1)} %copy-done, f32[8,4,128,128]{3,2,1,0:T(8,128)S(1)} %copy-done.1, s32[4,2,8,128]{3,2,1,0:T(8,128)S(1)} %copy-done.2, s32[4,8,128]{2,1,0:T(8,128)S(1)} %copy-done.3), custom_call_target="tpu_custom_call" | custom-call | tf_op jit(solution)/shard_map/matched_products/pallas_call | solution.py:234
Async XLA Ops:
  59.3 2.2 %copy-start = (f32[4,2,8,128,128]{4,3,2,1,0:T(8,128)S(1)}, f32[4,2,8,128,128]{4,3,2,1,0:T(8,128)}, u32[]{:S(2)}) copy-start(f32[4,2,8,128,128]{4,3,2,1,0:T(8,128)} %get-tuple-element.9.b_in) | copy-start | bytes 12582916
  61.5 1.6 %copy-start.1 = (f32[8,4,128,128]{3,2,1,0:T(8,128)S(1)}, f32[8,4,128,128]{3,2,1,0:T(8,128)}, u32[]{:S(2)}) copy-start(f32[8,4,128,128]{3,2,1,0:T(8,128)} %get-tuple-element.10.a_in) | copy-start | bytes 6291460
  63.1 0.8 copy-start.2
  63.9 0.7 copy-start.3
  64.6 0.7 copy-start.4
  65.2 0.7 copy-start.5

commit v2 on v0

v2 whole, which is shorter than its diff:
```python
import jax
import jax.numpy as jnp
from jax import lax
from jax.experimental import pallas as pl
from jax.experimental.pallas import tpu as pltpu
from jax.sharding import PartitionSpec as P

MESH = pl.DeviceIdType.MESH
BS = 128
SLOTS = 8
RB = 16
SECTIONS = 4
DEPTH = 4
F32 = jnp.float32
BF16 = jnp.bfloat16


def kernel(blocks, rows, cols, out, rows_v, cols_v, meta, mb, ma, mc, b0, b1, b2, a_all, c_down, c_in, acc,
           table, table_s, local_sem, ready, zs, zr, ys, yr, mzs, mzr, mys, myr, mus, mur,
           rs, rr, rms, rmr, gs, gr, cs, cr, out_sem):
    row, col = lax.axis_index("row"), lax.axis_index("col")
    z, yh = row // 2, row % 2
    other = 1 - yh
    x, yl, core = col // 4, (col // 2) % 2, col % 2
    row_below, row_above = (z + 15) % 16 * 2 + yh, (z + 1) % 16 * 2 + yh
    below, above = (row_below, col), (row_above, col)
    partner = (z * 2 + other, col)
    twin = (row, x * 4 + yl * 2 + 1 - core)
    section = (col + 16 - z) % 16
    chunk = x * 2 + core
    line = [(row, (x + d) % 4 * 4 + yl * 2 + core) for d in range(1, 4)]

    def remote(src, dst, send, recv, to):
        return pltpu.make_async_remote_copy(
            src_ref=src, dst_ref=dst, send_sem=send, recv_sem=recv, device_id=to, device_id_type=MESH
        )

    def signal(sem, to):
        pl.semaphore_signal(sem, inc=1, device_id=to, device_id_type=MESH)

    barrier = pltpu.get_barrier_semaphore()
    for to in (below, partner, twin, *line):
        signal(barrier, to)
    for s in range(3):
        @pl.when(section != s)
        def _():
            signal(barrier, (row, (z + s) % 16))
    signal(barrier, (row_below, (z + 2) % 16))

    own = pltpu.make_async_copy(blocks, b0.at[yh], local_sem.at[0])
    own.start()
    own_rows = pltpu.make_async_copy(rows, rows_v, local_sem.at[1])
    own_rows.start()
    own_cols = pltpu.make_async_copy(cols, cols_v, local_sem.at[2])
    own_cols.start()
    a_all[SLOTS] = jnp.zeros((SECTIONS, BS, BS), F32)
    meta[...] = jnp.full((8, BS), -1, jnp.int32)
    own_rows.wait()
    own_cols.wait()
    meta[0:1, 0:SLOTS] = rows_v[...]
    meta[1:2, 0:SLOTS] = cols_v[...]
    mb[0, yh] = meta[...]
    own.wait()

    pl.semaphore_wait(barrier, 6 + jnp.where(section < 3, 15, jnp.where(section == 3, 16, 0)))
    signal(ready, above)

    sends = []

    def go(copy):
        copy.start()
        sends.append(copy)

    go(remote(meta, mb.at[0, yh], mys.at[0], myr.at[0], partner))
    go(remote(meta, mc, mus, mur, above))
    for q in range(SLOTS):
        go(remote(b0.at[yh, q], b0.at[yh, q], ys.at[q], yr.at[q], partner))

    def root_copies(d, last):
        c = (col + d) % 16
        b = c // 4 * 2 + c % 2
        to = (row_above if last else row, c)
        s = SECTIONS - 1 if last else section
        return (
            remote(meta, ma.at[s], rms.at[d], rmr.at[s], to),
            remote(blocks.at[b], a_all.at[b, s], rs.at[d], rr.at[s], to),
        )

    def each_root_copy(act):
        @pl.when(section < 3)
        def _():
            for d in range(1, 16):
                for copy in root_copies(d, False):
                    act(copy)

        @pl.when(section == 3)
        def _():
            for d in range(16):
                for copy in root_copies(d, True):
                    act(copy)

    each_root_copy(lambda copy: copy.start())

    pl.semaphore_wait(ready, 1)
    go(remote(meta, mb.at[1, yh], mzs.at[0], mzr.at[0], below))
    for q in range(SLOTS):
        go(remote(b0.at[yh, q], b1.at[yh, q], zs.at[q], zr.at[q], below))

    @pl.when(section < 3)
    def _():
        mine = pltpu.make_async_copy(blocks.at[chunk], a_all.at[chunk, section], local_sem.at[3])
        mine.start()
        ma[section] = meta[...]
        mine.wait()

    remote(meta, mb.at[1, yh], mzs.at[0], mzr.at[0], below).wait_recv()
    go(remote(mb.at[1, yh], mb.at[2, yh], mzs.at[1], mzr.at[1], below))
    go(remote(mb.at[1, yh], mb.at[1, yh], mys.at[1], myr.at[1], partner))
    for q in range(SLOTS):
        remote(b0.at[yh, q], b1.at[yh, q], zs.at[q], zr.at[q], below).wait_recv()
        go(remote(b1.at[yh, q], b2.at[yh, q], zs.at[8 + q], zr.at[8 + q], below))
    remote(meta, mb.at[2, yh], mzs.at[1], mzr.at[1], below).wait_recv()
    go(remote(mb.at[2, yh], mb.at[2, yh], mys.at[2], myr.at[2], partner))

    for s in range(SECTIONS):
        def arrived():
            remote(meta, ma.at[s], rms.at[0], rmr.at[s], partner).wait_recv()
            remote(blocks.at[0], a_all.at[0, s], rs.at[0], rr.at[s], partner).wait_recv()

        if s < 3:
            pl.when(section != s)(arrived)
        else:
            arrived()
    for d in range(1, 4):
        go(remote(a_all.at[chunk], a_all.at[chunk], gs.at[d], gr.at[d], line[d - 1]))
    go(remote(a_all.at[chunk], a_all.at[chunk], cs.at[0], cr.at[0], twin))

    for q in range(SLOTS):
        remote(b1.at[yh, q], b2.at[yh, q], zs.at[8 + q], zr.at[8 + q], below).wait_recv()
        go(remote(b2.at[yh, q], b2.at[yh, q], ys.at[8 + q], yr.at[8 + q], partner))
    for q in range(SLOTS):
        go(remote(b1.at[yh, q], b1.at[yh, q], ys.at[16 + q], yr.at[16 + q], partner))
    for d in range(1, 4):
        b = (x + 4 - d) % 4 * 2 + core
        remote(a_all.at[b], a_all.at[b], gs.at[d], gr.at[d], twin).wait_recv()
        go(remote(a_all.at[b], a_all.at[b], cs.at[d], cr.at[d], twin))

    for i in range(3):
        remote(meta, mb.at[i, other], mys.at[i], myr.at[i], partner).wait_recv()
    remote(meta, mc, mus, mur, above).wait_recv()
    n = SLOTS
    lane = lax.broadcasted_iota(jnp.int32, (n, n), 1)
    diag = lax.broadcasted_iota(jnp.int32, (n, n), 0) == lane

    def upright(values):
        wide = jnp.broadcast_to(values, (n, n))
        return jnp.sum(jnp.where(diag, wide, 0), axis=1, keepdims=True)

    for s, (lists, i) in enumerate(((meta, 0), (meta, 1), (meta, 2), (mc, 2))):
        out_rows, out_cols = upright(lists[0:1, 0:n]), upright(lists[1:2, 0:n])
        a_rows, a_cols = ma[s, 0:1, 0:n], ma[s, 1:2, 0:n]
        same_row = (out_rows == a_rows) & (out_rows >= 0)
        found = jnp.full((n, n), -1, jnp.int32)
        for h in range(2):
            for q in range(n):
                inner, b_col = mb[i, h, 0:1, q:q + 1], mb[i, h, 1:2, q:q + 1]
                hit = (a_cols == inner + RB * h) & (out_cols == b_col) & (inner >= 0)
                found = jnp.where(hit, h * n + q, found)
        found = jnp.where(same_row, found, -1)
        matched = jnp.where(found >= 0, 1, 0)
        rank = jnp.zeros((n, n), jnp.int32)
        for p in range(n - 1):
            rank = rank + jnp.where(lane > p, matched[:, p:p + 1], 0)
        for d in range(DEPTH):
            pick = (matched > 0) & (rank == d)
            a_at = n + jnp.sum(jnp.where(pick, lane - n, 0), axis=1, keepdims=True)
            b_at = jnp.sum(jnp.where(pick, found, 0), axis=1, keepdims=True)
            table[s * n:(s + 1) * n, d:d + 1] = a_at
            table[s * n:(s + 1) * n, DEPTH + d:DEPTH + d + 1] = b_at
    to_scalars = pltpu.make_async_copy(table, table_s, local_sem.at[4])
    to_scalars.start()
    to_scalars.wait()

    for d in range(4):
        b = (x + 4 - d) % 4 * 2 + 1 - core
        remote(a_all.at[b], a_all.at[b], cs.at[d], cr.at[d], twin).wait_recv()

    def halves(v):
        high = v.astype(BF16)
        return high, (v - high.astype(F32)).astype(BF16)

    def product(s, t, b_ref):
        lefts, rights = [], []
        for d in range(DEPTH):
            a = a_all[table_s[s * n + t, d], s]
            at = table_s[s * n + t, DEPTH + d]
            b = b_ref[at // n, at % n]
            lefts += halves(a)
            wide = jnp.concatenate(halves(b), axis=1)
            rights += [wide, wide]
        both = jnp.dot(jnp.concatenate(lefts, axis=1), jnp.concatenate(rights, axis=0), preferred_element_type=F32)
        return both[:, :BS] + both[:, BS:]

    def partner_blocks(ref, first):
        for q in range(SLOTS):
            remote(ref.at[other, q], ref.at[other, q], ys.at[first + q], yr.at[first + q], partner).wait_recv()

    def down(t):
        return remote(c_down.at[t], c_in.at[t], zs.at[16 + t], zr.at[16 + t], below)

    partner_blocks(b2, 8)

    def last_section(t, carry):
        c_down[t] = product(3, t, b2)
        down(t).start()
        return carry

    lax.fori_loop(0, SLOTS, last_section, 0)
    partner_blocks(b0, 0)

    def early_sections(t, carry):
        acc[t] = product(0, t, b0) + product(2, t, b2)
        return carry

    lax.fori_loop(0, SLOTS, early_sections, 0)
    partner_blocks(b1, 16)

    def late_section(t, carry):
        acc[t] += product(1, t, b1)
        return carry

    lax.fori_loop(0, SLOTS, late_section, 0)

    def result(t):
        return pltpu.make_async_copy(acc.at[t], out.at[t], out_sem.at[t])

    def finish(t, carry):
        down(t).wait_recv()
        acc[t] += c_in[t]
        result(t).start()
        return carry

    lax.fori_loop(0, SLOTS, finish, 0)
    for t in range(SLOTS):
        down(t).wait_send()
    each_root_copy(lambda copy: copy.wait_send())
    for copy in sends:
        copy.wait_send()
    for t in range(SLOTS):
        result(t).wait()


def body(blocks, block_rows, block_cols):
    dma = pltpu.SemaphoreType.DMA
    hbm = pl.BlockSpec(memory_space=pl.ANY)
    tile = pltpu.VMEM((2, SLOTS, BS, BS), F32)
    lists = (8, BS)
    i32 = jnp.int32
    out = pl.pallas_call(
        kernel,
        out_shape=jax.ShapeDtypeStruct((SLOTS, BS, BS), F32),
        in_specs=[hbm, hbm, hbm],
        out_specs=hbm,
        scratch_shapes=[
            pltpu.VMEM((1, SLOTS), i32), pltpu.VMEM((1, SLOTS), i32),
            pltpu.VMEM(lists, i32), pltpu.VMEM((3, 2, *lists), i32), pltpu.VMEM((SECTIONS, *lists), i32),
            pltpu.VMEM(lists, i32),
            tile, tile, tile,
            pltpu.VMEM((SLOTS + 1, SECTIONS, BS, BS), F32),
            pltpu.VMEM((SLOTS, BS, BS), F32), pltpu.VMEM((SLOTS, BS, BS), F32), pltpu.VMEM((SLOTS, BS, BS), F32),
            pltpu.VMEM((SECTIONS * SLOTS, BS), i32), pltpu.SMEM((SECTIONS * SLOTS, BS), i32),
            dma((5,)), pltpu.SemaphoreType.REGULAR,
            dma((24,)), dma((24,)), dma((24,)), dma((24,)),
            dma((2,)), dma((2,)), dma((3,)), dma((3,)), dma(()), dma(()),
            dma((16,)), dma((4,)), dma((16,)), dma((4,)),
            dma((4,)), dma((4,)), dma((4,)), dma((4,)), dma((SLOTS,)),
        ],
        compiler_params=pltpu.CompilerParams(
            collective_id=0, has_side_effects=True, vmem_limit_bytes=32 * 2**20
        ),
        name="four_sections",
    )(blocks[0, 0], block_rows[0], block_cols[0])
    return out[None, None]


def solution(mesh):
    return jax.shard_map(
        body,
        mesh=mesh,
        in_specs=(P("row", "col", None, None, None), P("row", "col", None), P("row", "col", None)),
        out_specs=P("row", "col", None, None, None),
        check_vma=False,
    )
```

time: 245 us -> 63.1 us (0.26)
  waiting for transfers between devices: 126 us -> 0 us
  Pallas kernels: 0 us -> 60.4 us
  starting transfers between devices: 47.7 us -> 0 us
  local copies, waits for them, and re-layouts: 20.2 us -> 2.51 us
  matrix products: 14 us -> 0 us
  blocking collectives: 13.9 us -> 0 us
  between operations: 13.9 us -> 0.01 us
  other arithmetic: 8.89 us -> 0 us
    psum x1 -> x0, waiting for transfers between devices: 89.4 us -> none  [from_root(): return lax.psum(jnp.where(mine, x, jnp.zeros_like(x)), axis)]
    pallas_call x0 -> x1, Pallas kernels: none -> 60.4 us  [body(): pl.pallas_call(kernel, out_shape=jax.ShapeDtypeStruct((SLOTS, BS, BS), F3...]
    ppermute x12 -> x0, starting transfers between devices: 47.7 us -> none  [the longest x9 35.2 us: shifted(): return lax.ppermute(value, axis, pairs)]
    ppermute x12 -> x0, waiting for transfers between devices: 36.4 us -> none  [the longest x9 35.3 us: shifted(): return lax.ppermute(value, axis, pairs)]
    gather x8 -> x0, local copies, waits for them, and re-layouts: 18.5 us -> none  [the longest x4 9.31 us: section_product(): right = pair_vals[pair_slot]]
    dot_general x4 -> x0, matrix products: 14 us -> none  [section_product(): jnp.einsum('tqij,tqjk->tik', left, right, precision=lax.Precision.HIGHEST...]
    psum x1 -> x0, blocking collectives: 13.9 us -> none  [from_root(): return lax.psum(jnp.where(mine, x, jnp.zeros_like(x)), axis)]
    select_n x11 -> x0, other arithmetic: 3.8 us -> none  [the longest x1 2.44 us: from_root(): return lax.psum(jnp.where(mine, x, jnp.zeros_like(x)), axis)]
  transfers between devices with their start and end apart: 13 -> 0, of which waited for: 4 -> 0; matrix products, arithmetic and copies ran while one was open for 14% -> 0% of each run, Pallas kernels for 0% -> 0%
where the time goes in v2:
time: 63.1 us; the launch traced here: 63 us
  Pallas kernels  60.4 us (96%)
  local copies, waits for them, and re-layouts  2.51 us (4%)
    pallas_call x1, Pallas kernels, body(): pl.pallas_call(kernel, out_shape=jax.ShapeDtypeStruct((SLOTS, BS, BS), F3...  60.4 us
    unnamed x7, local copies, waits for them, and re-layouts  2.51 us

profile of v2, /device:TPU:1, one launch (start us, length us, event | category | flops | bytes accessed | tf_op | source)
XLA Modules:
  0.0 63.0 jit_solution(235605868290164175)
XLA Ops:
  0.0 0.0 copy-start.1
  0.0 0.0 copy-start.2
  0.0 0.7 %copy-done.1 = s32[1,1,8]{2,1,0:T(1,128)S(1)} copy-done((s32[1,1,8]{2,1,0:T(1,128)S(1)}, s32[1,1,8]{2,1,0:T(1,128)}, u32[]{:S(2)}) %copy-start.1) | copy-done | bytes 56
  0.7 0.0 copy-done.2
  0.7 0.0 copy-start
  0.7 1.0 %copy-done = f32[1,1,8,128,128]{4,3,2,1,0:T(8,128)S(1)} copy-done((f32[1,1,8,128,128]{4,3,2,1,0:T(8,128)S(1)}, f32[1,1,8,128,128]{4,3,2,1,0:T(8,128)}, u32[]{:S(2)}) %copy-start) | copy-done | bytes 524312
  1.7 60.4 %four_sections.1 = f32[8,128,128]{2,1,0:T(8,128)S(1)} custom-call(f32[8,128,128]{2,1,0:T(8,128)S(1)} %bitcast.5, s32[1,8]{1,0:T(1,128)S(1)} %bitcast.6, s32[1,8]{1,0:T(1,128)S(1)} %bitcast.7), custom_call_target="tpu_custom_call" | custom-call | tf_op jit(solution)/shard_map/four_sections/pallas_call | solution.py:259
  62.2 0.8 %copy.5 = f32[1,1,8,128,128]{4,3,2,1,0:T(8,128)} copy(f32[1,1,8,128,128]{4,3,2,1,0:T(8,128)S(1)} %bitcast.4) | data formatting | bytes 1048576
Async XLA Ops:
  0.0 0.7 %copy-start.1 = (s32[1,1,8]{2,1,0:T(1,128)S(1)}, s32[1,1,8]{2,1,0:T(1,128)}, u32[]{:S(2)}) copy-start(s32[1,1,8]{2,1,0:T(1,128)} %param.4) | copy-start | bytes 100
  0.0 0.7 %copy-start.2 = (s32[1,1,8]{2,1,0:T(1,128)S(1)}, s32[1,1,8]{2,1,0:T(1,128)}, u32[]{:S(2)}) copy-start(s32[1,1,8]{2,1,0:T(1,128)} %param.5) | copy-start | bytes 100
  0.7 1.0 %copy-start = (f32[1,1,8,128,128]{4,3,2,1,0:T(8,128)S(1)}, f32[1,1,8,128,128]{4,3,2,1,0:T(8,128)}, u32[]{:S(2)}) copy-start(f32[1,1,8,128,128]{4,3,2,1,0:T(8,128)} %param.3) | copy-start | bytes 1572868

commit v3 on v2

v3 whole, which is shorter than its diff:
```python
import jax
import jax.numpy as jnp
from jax import lax
from jax.experimental import pallas as pl
from jax.experimental.pallas import tpu as pltpu
from jax.sharding import PartitionSpec as P

MESH = pl.DeviceIdType.MESH
BS = 128
SLOTS = 8
RB = 16
SECTIONS = 4
DEPTH = 4
EARLY = 2
F32 = jnp.float32
BF16 = jnp.bfloat16


def kernel(blocks, rows, cols, out, rows_v, cols_v, meta, mb, ma, mc, b0, b1, b2, a_last, a_mid, a_first, c_down, c_in, acc,
           table, table_s, local_sem, ready, zs, zr, ys, yr, mzs, mzr, mys, myr, mus, mur,
           rs, rr, rms, rmr, ks, kr, gs, gr, cs, cr, out_sem):
    row, col = lax.axis_index("row"), lax.axis_index("col")
    z, yh = row // 2, row % 2
    other = 1 - yh
    x, yl, core = col // 4, (col // 2) % 2, col % 2
    row_below, row_above = (z + 15) % 16 * 2 + yh, (z + 1) % 16 * 2 + yh
    below, above = (row_below, col), (row_above, col)
    partner = (z * 2 + other, col)
    twin = (row, x * 4 + yl * 2 + 1 - core)
    opposite = (row, x * 4 + (1 - yl) * 2 + core)
    section = (col + 16 - z) % 16
    chunk = x * 2 + core
    line = [(row, (x + d) % 4 * 4 + yl * 2 + core) for d in range(1, 4)]

    def remote(src, dst, send, recv, to):
        return pltpu.make_async_remote_copy(
            src_ref=src, dst_ref=dst, send_sem=send, recv_sem=recv, device_id=to, device_id_type=MESH
        )

    def signal(sem, to):
        pl.semaphore_signal(sem, inc=1, device_id=to, device_id_type=MESH)

    barrier = pltpu.get_barrier_semaphore()
    for to in (below, partner, twin, opposite, *line):
        signal(barrier, to)
    for s in range(3):
        @pl.when(section != s)
        def _():
            signal(barrier, (row, (z + s) % 16))
    signal(barrier, (row_below, (z + 2) % 16))

    own = pltpu.make_async_copy(blocks, b0.at[yh], local_sem.at[0])
    own.start()
    own_rows = pltpu.make_async_copy(rows, rows_v, local_sem.at[1])
    own_rows.start()
    own_cols = pltpu.make_async_copy(cols, cols_v, local_sem.at[2])
    own_cols.start()
    for ref in (a_last, a_mid, a_first):
        ref[SLOTS] = jnp.zeros(ref.shape[1:], F32)
    meta[...] = jnp.full((8, BS), -1, jnp.int32)
    own_rows.wait()
    own_cols.wait()
    meta[0:1, 0:SLOTS] = rows_v[...]
    meta[1:2, 0:SLOTS] = cols_v[...]
    mb[0, yh] = meta[...]
    own.wait()

    pl.semaphore_wait(barrier, 7 + jnp.where(section < 3, 15, jnp.where(section == 3, 16, 0)))
    signal(ready, above)

    sends = [], [], []

    def go(copy, when=0):
        copy.start()
        sends[when].append(copy)

    def across(ref, q, first, when=0):
        go(remote(ref.at[yh, q], ref.at[yh, q], ys.at[first + q], yr.at[first + q], partner), when)

    go(remote(meta, mb.at[0, yh], mys.at[0], myr.at[0], partner))
    go(remote(meta, mc, mus, mur, above))
    for q in range(3):
        across(b0, q, 0)

    panels = a_last, a_mid, a_first
    places = (2, 0), (1, 0), (1, 1), (0, 0)
    holders = section == 3, (section == 1) | (section == 2), section == 0

    def panel(b, s):
        return panels[places[s][0]].at[b, places[s][1]]

    def root_copies(b, g):
        c = b // 2 * 4 + yl * 2 + b % 2
        to = (row_above if g == 0 else row, c)
        return remote(blocks.at[b], panels[g].at[b, section - 1 if g == 1 else 0], rs.at[b], rr.at[section], to)

    def root_lists(d, last):
        s = SECTIONS - 1 if last else section
        return remote(meta, ma.at[s], rms.at[d], rmr.at[s], (row_above if last else row, (col + d) % 16))

    def each_root_copy(act):
        for g in range(3):
            @pl.when(holders[g])
            def _():
                for d in range(0 if g == 0 else 1, SLOTS):
                    act(root_copies((chunk + d) % SLOTS, g))

    def each_root_list(act):
        @pl.when(section < 3)
        def _():
            for d in range(1, 16):
                act(root_lists(d, False))

        @pl.when(section == 3)
        def _():
            for d in range(16):
                act(root_lists(d, True))

    each_root_list(lambda copy: copy.start())
    each_root_copy(lambda copy: copy.start())

    pl.semaphore_wait(ready, 1)
    go(remote(meta, mb.at[1, yh], mzs.at[0], mzr.at[0], below))
    for q in range(SLOTS):
        go(remote(b0.at[yh, q], b1.at[yh, q], zs.at[q], zr.at[q], below))

    for g in (1, 2):
        @pl.when(holders[g])
        def _():
            at = panels[g].at[chunk, section - 1 if g == 1 else 0]
            mine = pltpu.make_async_copy(blocks.at[chunk], at, local_sem.at[3])
            mine.start()
            ma[section] = meta[...]
            mine.wait()

    def from_here(s):
        return ((z + s) % 16 if s < 3 else (z + 2) % 16) // 2 % 2 == yl

    def cross(s):
        return remote(panel(chunk, s), panel(chunk, s), ks.at[s], kr.at[s], opposite)

    def panel_lists(s):
        def arrived():
            remote(meta, ma.at[s], rms.at[0], rmr.at[s], partner).wait_recv()

        if s < 3:
            pl.when(section != s)(arrived)
        else:
            arrived()

    def panel_cross(s):
        @pl.when(from_here(s))
        def _():
            def arrived():
                remote(blocks.at[0], panel(0, s), rs.at[0], rr.at[s], partner).wait_recv()

            if s < 3:
                pl.when(section != s)(arrived)
            else:
                arrived()
            cross(s).start()

    def part(b, g):
        return panels[g].at[b]

    def panel_spread(g):
        for s in ((3,), (1, 2), (0,))[g]:
            @pl.when(jnp.logical_not(from_here(s)))
            def _():
                cross(s).wait_recv()
        for d in range(1, 4):
            go(remote(part(chunk, g), part(chunk, g), gs.at[g, d], gr.at[g, d], line[d - 1]), g)
        go(remote(part(chunk, g), part(chunk, g), cs.at[g, 0], cr.at[g, 0], twin), g)

    def panel_twin(g):
        for d in range(1, 4):
            b = (x + 4 - d) % 4 * 2 + core
            remote(part(b, g), part(b, g), gs.at[g, d], gr.at[g, d], twin).wait_recv()
            go(remote(part(b, g), part(b, g), cs.at[g, d], cr.at[g, d], twin), g)

    def panel_whole(g):
        for d in range(4):
            b = (x + 4 - d) % 4 * 2 + 1 - core
            remote(part(b, g), part(b, g), cs.at[g, d], cr.at[g, d], twin).wait_recv()

    def partner_block(ref, q, first):
        remote(ref.at[other, q], ref.at[other, q], ys.at[first + q], yr.at[first + q], partner).wait_recv()

    def from_both(q):
        return remote(b1.at[other, q], b2.at[other, q], zs.at[24 + q], zr.at[24 + q], below)

    n = SLOTS
    to_scalars = pltpu.make_async_copy(table, table_s, local_sem.at[4])

    def match():
        for i in range(3):
            remote(meta, mb.at[i, other], mys.at[i], myr.at[i], partner).wait_recv()
        remote(meta, mc, mus, mur, above).wait_recv()
        for s in range(SECTIONS):
            panel_lists(s)
        lane = lax.broadcasted_iota(jnp.int32, (n, n), 1)
        diag = lax.broadcasted_iota(jnp.int32, (n, n), 0) == lane

        def upright(values):
            wide = jnp.broadcast_to(values, (n, n))
            return jnp.sum(jnp.where(diag, wide, 0), axis=1, keepdims=True)

        for s, (lists, i) in enumerate(((meta, 0), (meta, 1), (meta, 2), (mc, 2))):
            out_rows, out_cols = upright(lists[0:1, 0:n]), upright(lists[1:2, 0:n])
            a_rows, a_cols = ma[s, 0:1, 0:n], ma[s, 1:2, 0:n]
            same_row = (out_rows == a_rows) & (out_rows >= 0)
            found = jnp.full((n, n), -1, jnp.int32)
            for h in range(2):
                for q in range(n):
                    inner, b_col = mb[i, h, 0:1, q:q + 1], mb[i, h, 1:2, q:q + 1]
                    hit = (a_cols == inner + RB * h) & (out_cols == b_col) & (inner >= 0)
                    found = jnp.where(hit, h * n + q, found)
            found = jnp.where(same_row, found, -1)
            matched = jnp.where(found >= 0, 1, 0)
            rank = jnp.zeros((n, n), jnp.int32)
            for p in range(n - 1):
                rank = rank + jnp.where(lane > p, matched[:, p:p + 1], 0)
            for d in range(DEPTH):
                pick = (matched > 0) & (rank == d)
                a_at = n + jnp.sum(jnp.where(pick, lane - n, 0), axis=1, keepdims=True)
                b_at = jnp.sum(jnp.where(pick, found, 0), axis=1, keepdims=True)
                table[s * n:(s + 1) * n, d:d + 1] = a_at
                table[s * n:(s + 1) * n, DEPTH + d:DEPTH + d + 1] = b_at
        to_scalars.start()

    remote(meta, mb.at[1, yh], mzs.at[0], mzr.at[0], below).wait_recv()
    go(remote(mb.at[1, yh], mb.at[2, yh], mzs.at[1], mzr.at[1], below))
    go(remote(mb.at[1, yh], mb.at[1, yh], mys.at[1], myr.at[1], partner))
    for q in range(SLOTS):
        remote(b0.at[yh, q], b1.at[yh, q], zs.at[q], zr.at[q], below).wait_recv()
        go(remote(b1.at[yh, q], b2.at[yh, q], zs.at[8 + q], zr.at[8 + q], below), 1)
        if q < EARLY:
            across(b1, q, 16)
        if q == 4:
            panel_cross(3)
        elif EARLY <= q < 7:
            across(b0, q + (1 if q < 4 else 0), 0)
    remote(meta, mb.at[2, yh], mzs.at[1], mzr.at[1], below).wait_recv()
    go(remote(mb.at[2, yh], mb.at[2, yh], mys.at[2], myr.at[2], partner))
    panel_spread(0)
    panel_cross(2)
    panel_cross(1)

    for q in range(SLOTS):
        remote(b1.at[yh, q], b2.at[yh, q], zs.at[8 + q], zr.at[8 + q], below).wait_recv()
        if q >= EARLY:
            across(b2, q, 8, 1)
        if q == 0:
            across(b0, 7, 0, 1)
        if q == 2:
            match()
        if q == 3:
            panel_spread(1)
            panel_cross(0)
        if q == 4:
            panel_twin(0)
    for q in range(EARLY):
        partner_block(b1, q, 16)
        go(from_both(q), 1)
    for q in range(EARLY, SLOTS):
        across(b1, q, 16, 2)
    panel_spread(2)
    panel_whole(0)
    to_scalars.wait()

    def halves(v):
        high = v.astype(BF16)
        return high, (v - high.astype(F32)).astype(BF16)

    def product(s, t, b_ref):
        lefts, rights = [], []
        for d in range(DEPTH):
            a = panels[places[s][0]][table_s[s * n + t, d], places[s][1]]
            at = table_s[s * n + t, DEPTH + d]
            b = b_ref[at // n, at % n]
            lefts += halves(a)
            wide = jnp.concatenate(halves(b), axis=1)
            rights += [wide, wide]
        both = jnp.dot(jnp.concatenate(lefts, axis=1), jnp.concatenate(rights, axis=0), preferred_element_type=F32)
        return both[:, :BS] + both[:, BS:]

    def down(t):
        return remote(c_down.at[t], c_in.at[t], zs.at[16 + t], zr.at[16 + t], below)

    def sent(when):
        for copy in sends[when]:
            copy.wait_send()

    each_root_list(lambda copy: copy.wait_send())
    each_root_copy(lambda copy: copy.wait_send())
    sent(0)
    for q in range(EARLY, SLOTS):
        partner_block(b2, q, 8)
    for q in range(EARLY):
        from_both(q).wait_recv()

    def last_section(t, carry):
        c_down[t] = product(3, t, b2)
        down(t).start()
        return carry

    lax.fori_loop(0, SLOTS, last_section, 0)
    panel_twin(1)
    panel_whole(1)

    def section_two(t, carry):
        acc[t] = product(2, t, b2)
        return carry

    lax.fori_loop(0, SLOTS, section_two, 0)
    panel_twin(2)
    panel_whole(2)
    for q in range(SLOTS):
        partner_block(b0, q, 0)

    def section_zero(t, carry):
        acc[t] += product(0, t, b0)
        return carry

    lax.fori_loop(0, SLOTS, section_zero, 0)
    for s in range(SECTIONS):
        @pl.when(from_here(s))
        def _():
            cross(s).wait_send()
    sent(1)
    for q in range(EARLY, SLOTS):
        partner_block(b1, q, 16)

    def section_one(t, carry):
        acc[t] += product(1, t, b1)
        return carry

    lax.fori_loop(0, SLOTS, section_one, 0)

    def result(t):
        return pltpu.make_async_copy(acc.at[t], out.at[t], out_sem.at[t])

    def finish(t, carry):
        down(t).wait_recv()
        acc[t] += c_in[t]
        result(t).start()
        return carry

    lax.fori_loop(0, SLOTS, finish, 0)
    for t in range(SLOTS):
        down(t).wait_send()
    sent(2)
    for t in range(SLOTS):
        result(t).wait()


def body(blocks, block_rows, block_cols):
    dma = pltpu.SemaphoreType.DMA
    hbm = pl.BlockSpec(memory_space=pl.ANY)
    tile = pltpu.VMEM((2, SLOTS, BS, BS), F32)
    lists = (8, BS)
    i32 = jnp.int32
    out = pl.pallas_call(
        kernel,
        out_shape=jax.ShapeDtypeStruct((SLOTS, BS, BS), F32),
        in_specs=[hbm, hbm, hbm],
        out_specs=hbm,
        scratch_shapes=[
            pltpu.VMEM((1, SLOTS), i32), pltpu.VMEM((1, SLOTS), i32),
            pltpu.VMEM(lists, i32), pltpu.VMEM((3, 2, *lists), i32), pltpu.VMEM((SECTIONS, *lists), i32),
            pltpu.VMEM(lists, i32),
            tile, tile, tile,
            *(pltpu.VMEM((SLOTS + 1, m, BS, BS), F32) for m in (1, 2, 1)),
            pltpu.VMEM((SLOTS, BS, BS), F32), pltpu.VMEM((SLOTS, BS, BS), F32), pltpu.VMEM((SLOTS, BS, BS), F32),
            pltpu.VMEM((SECTIONS * SLOTS, BS), i32), pltpu.SMEM((SECTIONS * SLOTS, BS), i32),
            dma((5,)), pltpu.SemaphoreType.REGULAR,
            dma((32,)), dma((32,)), dma((24,)), dma((24,)),
            dma((2,)), dma((2,)), dma((3,)), dma((3,)), dma(()), dma(()),
            dma((SLOTS,)), dma((4,)), dma((16,)), dma((4,)), dma((4,)), dma((4,)),
            dma((3, 4)), dma((3, 4)), dma((3, 4)), dma((3, 4)), dma((SLOTS,)),
        ],
        compiler_params=pltpu.CompilerParams(
            collective_id=0, has_side_effects=True, vmem_limit_bytes=56 * 2**20
        ),
        name="four_sections",
    )(blocks[0, 0], block_rows[0], block_cols[0])
    return out[None, None]


def solution(mesh):
    return jax.shard_map(
        body,
        mesh=mesh,
        in_specs=(P("row", "col", None, None, None), P("row", "col", None), P("row", "col", None)),
        out_specs=P("row", "col", None, None, None),
        check_vma=False,
    )
```

time: 63.1 us -> 57.9 us (0.918)
  the two profiles are of different devices: /device:TPU:1 before, /device:TPU:7 now
where the time goes in v3:
time: 57.9 us; the launch traced here: 57.7 us
  Pallas kernels  55.8 us (96%)
  local copies, waits for them, and re-layouts  1.87 us (3%)
    pallas_call x1, Pallas kernels, body(): pl.pallas_call(kernel, out_shape=jax.ShapeDtypeStruct((SLOTS, BS, BS), F3...  55.8 us
    unnamed x1, local copies, waits for them, and re-layouts  1.87 us

profile of v3, /device:TPU:7, one launch (start us, length us, event | category | flops | bytes accessed | tf_op | source)
XLA Modules:
  0.0 57.7 jit_solution(6890565500213401530)
XLA Ops:
  0.0 55.8 %four_sections.1 = f32[8,128,128]{2,1,0:T(8,128)} custom-call(f32[8,128,128]{2,1,0:T(8,128)} %bitcast.5, s32[1,8]{1,0:T(1,128)} %bitcast.6, s32[1,8]{1,0:T(1,128)} %bitcast.7), custom_call_target="tpu_custom_call" | custom-call | tf_op jit(solution)/shard_map/four_sections/pallas_call | solution.py:363
  55.8 1.9 %copy.5 = f32[1,1,8,128,128]{4,3,2,1,0:T(8,128)} copy(f32[1,1,8,128,128]{4,3,2,1,0:T(8,128)} %bitcast.4) | data formatting | bytes 1048576

commit v4 on v3

--- a/solution.py
+++ b/solution.py
@@ -236,13 +236,12 @@
         go(remote(b1.at[yh, q], b2.at[yh, q], zs.at[8 + q], zr.at[8 + q], below), 1)
         if q < EARLY:
             across(b1, q, 16)
-        if q == 4:
+        if q == 6:
             panel_cross(3)
-        elif EARLY <= q < 7:
-            across(b0, q + (1 if q < 4 else 0), 0)
+        elif EARLY <= q:
+            across(b0, q + (1 if q < 6 else 0), 0)
     remote(meta, mb.at[2, yh], mzs.at[1], mzr.at[1], below).wait_recv()
     go(remote(mb.at[2, yh], mb.at[2, yh], mys.at[2], myr.at[2], partner))
-    panel_spread(0)
     panel_cross(2)
     panel_cross(1)
 
@@ -250,21 +249,20 @@
         remote(b1.at[yh, q], b2.at[yh, q], zs.at[8 + q], zr.at[8 + q], below).wait_recv()
         if q >= EARLY:
             across(b2, q, 8, 1)
-        if q == 0:
-            across(b0, 7, 0, 1)
         if q == 2:
             match()
         if q == 3:
+            panel_spread(0)
+        if q == 4:
             panel_spread(1)
             panel_cross(0)
-        if q == 4:
-            panel_twin(0)
     for q in range(EARLY):
         partner_block(b1, q, 16)
         go(from_both(q), 1)
     for q in range(EARLY, SLOTS):
         across(b1, q, 16, 2)
     panel_spread(2)
+    panel_twin(0)
     panel_whole(0)
     to_scalars.wait()
 
@@ -299,30 +297,26 @@
     for q in range(EARLY):
         from_both(q).wait_recv()
 
-    def last_section(t, carry):
-        c_down[t] = product(3, t, b2)
-        down(t).start()
+    def last_section(i, carry):
+        c_down[2 * i], c_down[2 * i + 1] = product(3, 2 * i, b2), product(3, 2 * i + 1, b2)
+        down(2 * i).start()
+        down(2 * i + 1).start()
         return carry
 
-    lax.fori_loop(0, SLOTS, last_section, 0)
+    lax.fori_loop(0, SLOTS // 2, last_section, 0)
     panel_twin(1)
     panel_whole(1)
 
-    def section_two(t, carry):
-        acc[t] = product(2, t, b2)
+    def section_two(i, carry):
+        acc[2 * i], acc[2 * i + 1] = product(2, 2 * i, b2), product(2, 2 * i + 1, b2)
         return carry
 
-    lax.fori_loop(0, SLOTS, section_two, 0)
+    lax.fori_loop(0, SLOTS // 2, section_two, 0)
     panel_twin(2)
     panel_whole(2)
     for q in range(SLOTS):
         partner_block(b0, q, 0)
 
-    def section_zero(t, carry):
-        acc[t] += product(0, t, b0)
-        return carry
-
-    lax.fori_loop(0, SLOTS, section_zero, 0)
     for s in range(SECTIONS):
         @pl.when(from_here(s))
         def _():
@@ -331,11 +325,11 @@
     for q in range(EARLY, SLOTS):
         partner_block(b1, q, 16)
 
-    def section_one(t, carry):
-        acc[t] += product(1, t, b1)
+    def sections_zero_one(t, carry):
+        acc[t] += product(0, t, b0) + product(1, t, b1)
         return carry
 
-    lax.fori_loop(0, SLOTS, section_one, 0)
+    lax.fori_loop(0, SLOTS, sections_zero_one, 0)
 
     def result(t):
         return pltpu.make_async_copy(acc.at[t], out.at[t], out_sem.at[t])
@@ -380,7 +374,7 @@
             dma((3, 4)), dma((3, 4)), dma((3, 4)), dma((3, 4)), dma((SLOTS,)),
         ],
         compiler_params=pltpu.CompilerParams(
-            collective_id=0, has_side_effects=True, vmem_limit_bytes=56 * 2**20
+            collective_id=0, has_side_effects=True, vmem_limit_bytes=53 * 2**20
         ),
         name="four_sections",
     )(blocks[0, 0], block_rows[0], block_cols[0])

time: 57.9 us -> 55.5 us (0.959)
  the two profiles are of different devices: /device:TPU:7 before, /device:TPU:1 now
where the time goes in v4:
time: 55.5 us; the launch traced here: 55.3 us
  Pallas kernels  53.8 us (97%)
  local copies, waits for them, and re-layouts  1.47 us (3%)
    pallas_call x1, Pallas kernels, body(): pl.pallas_call(kernel, out_shape=jax.ShapeDtypeStruct((SLOTS, BS, BS), F3...  53.8 us
    unnamed x5, local copies, waits for them, and re-layouts  1.47 us

profile of v4, /device:TPU:1, one launch (start us, length us, event | category | flops | bytes accessed | tf_op | source)
XLA Modules:
  0.0 55.3 jit_solution(15537781903630821657)
XLA Ops:
  0.0 0.0 copy-start
  0.0 0.0 copy-start.1
  0.0 0.7 %copy-done = s32[1,1,8]{2,1,0:T(1,128)S(1)} copy-done((s32[1,1,8]{2,1,0:T(1,128)S(1)}, s32[1,1,8]{2,1,0:T(1,128)}, u32[]{:S(2)}) %copy-start) | copy-done | bytes 56
  0.7 0.0 copy-done.1
  0.7 53.8 %four_sections.1 = f32[8,128,128]{2,1,0:T(8,128)S(1)} custom-call(f32[8,128,128]{2,1,0:T(8,128)} %bitcast.7, s32[1,8]{1,0:T(1,128)S(1)} %bitcast.5, s32[1,8]{1,0:T(1,128)S(1)} %bitcast.6), custom_call_target="tpu_custom_call" | custom-call | tf_op jit(solution)/shard_map/four_sections/pallas_call | solution.py:357
  54.5 0.8 %copy.5 = f32[1,1,8,128,128]{4,3,2,1,0:T(8,128)} copy(f32[1,1,8,128,128]{4,3,2,1,0:T(8,128)S(1)} %bitcast.4) | data formatting | bytes 1048576
Async XLA Ops:
  0.0 0.7 %copy-start = (s32[1,1,8]{2,1,0:T(1,128)S(1)}, s32[1,1,8]{2,1,0:T(1,128)}, u32[]{:S(2)}) copy-start(s32[1,1,8]{2,1,0:T(1,128)} %param.4) | copy-start | bytes 100
  0.0 0.7 %copy-start.1 = (s32[1,1,8]{2,1,0:T(1,128)S(1)}, s32[1,1,8]{2,1,0:T(1,128)}, u32[]{:S(2)}) copy-start(s32[1,1,8]{2,1,0:T(1,128)} %param.5) | copy-start | bytes 100

commit v5 on v4

--- a/solution.py
+++ b/solution.py
@@ -238,8 +238,8 @@
             across(b1, q, 16)
         if q == 6:
             panel_cross(3)
-        elif EARLY <= q:
-            across(b0, q + (1 if q < 6 else 0), 0)
+        elif EARLY <= q < EARLY + 4:
+            across(b0, q + 1, 0)
     remote(meta, mb.at[2, yh], mzs.at[1], mzr.at[1], below).wait_recv()
     go(remote(mb.at[2, yh], mb.at[2, yh], mys.at[2], myr.at[2], partner))
     panel_cross(2)
@@ -261,6 +261,7 @@
         go(from_both(q), 1)
     for q in range(EARLY, SLOTS):
         across(b1, q, 16, 2)
+    across(b0, SLOTS - 1, 0, 2)
     panel_spread(2)
     panel_twin(0)
     panel_whole(0)
@@ -325,11 +326,15 @@
     for q in range(EARLY, SLOTS):
         partner_block(b1, q, 16)
 
-    def sections_zero_one(t, carry):
-        acc[t] += product(0, t, b0) + product(1, t, b1)
+    def sections_zero_one(i, carry):
+        first, second = 2 * i, 2 * i + 1
+        acc[first], acc[second] = (
+            acc[first] + product(0, first, b0) + product(1, first, b1),
+            acc[second] + product(0, second, b0) + product(1, second, b1),
+        )
         return carry
 
-    lax.fori_loop(0, SLOTS, sections_zero_one, 0)
+    lax.fori_loop(0, SLOTS // 2, sections_zero_one, 0)
 
     def result(t):
         return pltpu.make_async_copy(acc.at[t], out.at[t], out_sem.at[t])

time: 55.5 us -> 55.3 us (level)
  the two profiles are of different devices: /device:TPU:1 before, /device:TPU:2 now
where the time goes in v5:
time: 55.3 us; the launch traced here: 55.1 us
  Pallas kernels  53.6 us (97%)
  local copies, waits for them, and re-layouts  1.47 us (3%)
    pallas_call x1, Pallas kernels, body(): pl.pallas_call(kernel, out_shape=jax.ShapeDtypeStruct((SLOTS, BS, BS), F3...  53.6 us
    unnamed x5, local copies, waits for them, and re-layouts  1.47 us

profile of v5, /device:TPU:2, one launch (start us, length us, event | category | flops | bytes accessed | tf_op | source)
XLA Modules:
  0.0 55.1 jit_solution(13533595936733429844)
XLA Ops:
  0.0 0.0 copy-start
  0.0 0.0 copy-start.1
  0.0 0.7 %copy-done = s32[1,1,8]{2,1,0:T(1,128)S(1)} copy-done((s32[1,1,8]{2,1,0:T(1,128)S(1)}, s32[1,1,8]{2,1,0:T(1,128)}, u32[]{:S(2)}) %copy-start) | copy-done | bytes 56
  0.7 0.0 copy-done.1
  0.7 53.6 %four_sections.1 = f32[8,128,128]{2,1,0:T(8,128)S(1)} custom-call(f32[8,128,128]{2,1,0:T(8,128)} %bitcast.7, s32[1,8]{1,0:T(1,128)S(1)} %bitcast.5, s32[1,8]{1,0:T(1,128)S(1)} %bitcast.6), custom_call_target="tpu_custom_call" | custom-call | tf_op jit(solution)/shard_map/four_sections/pallas_call | solution.py:362
  54.3 0.8 %copy.5 = f32[1,1,8,128,128]{4,3,2,1,0:T(8,128)} copy(f32[1,1,8,128,128]{4,3,2,1,0:T(8,128)S(1)} %bitcast.4) | data formatting | bytes 1048576
Async XLA Ops:
  0.0 0.7 %copy-start = (s32[1,1,8]{2,1,0:T(1,128)S(1)}, s32[1,1,8]{2,1,0:T(1,128)}, u32[]{:S(2)}) copy-start(s32[1,1,8]{2,1,0:T(1,128)} %param.4) | copy-start | bytes 100
  0.0 0.7 %copy-start.1 = (s32[1,1,8]{2,1,0:T(1,128)S(1)}, s32[1,1,8]{2,1,0:T(1,128)}, u32[]{:S(2)}) copy-start(s32[1,1,8]{2,1,0:T(1,128)} %param.5) | copy-start | bytes 100

commit v6 on v5

--- a/solution.py
+++ b/solution.py
@@ -314,15 +314,15 @@
 
     lax.fori_loop(0, SLOTS // 2, section_two, 0)
     panel_twin(2)
+    for s in range(SECTIONS):
+        @pl.when(from_here(s))
+        def _():
+            cross(s).wait_send()
+    sent(1)
     panel_whole(2)
     for q in range(SLOTS):
         partner_block(b0, q, 0)
 
-    for s in range(SECTIONS):
-        @pl.when(from_here(s))
-        def _():
-            cross(s).wait_send()
-    sent(1)
     for q in range(EARLY, SLOTS):
         partner_block(b1, q, 16)
 

time: 55.3 us -> 55.3 us (level)
  no operation moved by 1% of the time
where the time goes in v6:
time: 55.3 us; the launch traced here: 55.1 us
  Pallas kernels  53.6 us (97%)
  local copies, waits for them, and re-layouts  1.47 us (3%)
    pallas_call x1, Pallas kernels, body(): pl.pallas_call(kernel, out_shape=jax.ShapeDtypeStruct((SLOTS, BS, BS), F3...  53.6 us
    unnamed x5, local copies, waits for them, and re-layouts  1.47 us

profile of v6, /device:TPU:2, one launch (start us, length us, event | category | flops | bytes accessed | tf_op | source)
XLA Modules:
  0.0 55.1 jit_solution(11411192567359938903)
XLA Ops:
  0.0 0.0 copy-start
  0.0 0.0 copy-start.1
  0.0 0.7 %copy-done = s32[1,1,8]{2,1,0:T(1,128)S(1)} copy-done((s32[1,1,8]{2,1,0:T(1,128)S(1)}, s32[1,1,8]{2,1,0:T(1,128)}, u32[]{:S(2)}) %copy-start) | copy-done | bytes 56
  0.7 0.0 copy-done.1
  0.7 53.6 %four_sections.1 = f32[8,128,128]{2,1,0:T(8,128)S(1)} custom-call(f32[8,128,128]{2,1,0:T(8,128)} %bitcast.7, s32[1,8]{1,0:T(1,128)S(1)} %bitcast.5, s32[1,8]{1,0:T(1,128)S(1)} %bitcast.6), custom_call_target="tpu_custom_call" | custom-call | tf_op jit(solution)/shard_map/four_sections/pallas_call | solution.py:362
  54.3 0.8 %copy.5 = f32[1,1,8,128,128]{4,3,2,1,0:T(8,128)} copy(f32[1,1,8,128,128]{4,3,2,1,0:T(8,128)S(1)} %bitcast.4) | data formatting | bytes 1048576
Async XLA Ops:
  0.0 0.7 %copy-start = (s32[1,1,8]{2,1,0:T(1,128)S(1)}, s32[1,1,8]{2,1,0:T(1,128)}, u32[]{:S(2)}) copy-start(s32[1,1,8]{2,1,0:T(1,128)} %param.4) | copy-start | bytes 100
  0.0 0.7 %copy-start.1 = (s32[1,1,8]{2,1,0:T(1,128)S(1)}, s32[1,1,8]{2,1,0:T(1,128)}, u32[]{:S(2)}) copy-start(s32[1,1,8]{2,1,0:T(1,128)} %param.5) | copy-start | bytes 100
